TPU v7x, 32 devices: a whole 2x2x4 slice. The times are simulated.
32 devices in a mesh: row: 8 (over y, x, core), col: 4 (over z).
Axes of the slice: x: 2, y: 2, z: 4, core: 2. Of those that a mesh axis runs over, the one named last changes fastest.
Arguments:
- tokens: bfloat16 [512, 8192], P('col', 'row'), may hold values from -6 to 6
- cotangent: bfloat16 [512, 8192], P('col', 'row'), may hold values from -6 to 6
- gate_weight: bfloat16 [8192, 28672], P('row', 'col'), may hold values from -0.09375 to 0.09375
- up_weight: bfloat16 [8192, 28672], P('row', 'col'), may hold values from -0.09375 to 0.09375
- down_weight: bfloat16 [28672, 8192], P('col', 'row'), may hold values from -0.0625 to 0.0625
- gate_mask: int32 [64, 224], P('row', 'col'), may hold values 0 or 1
- up_mask: int32 [64, 224], P('row', 'col'), may hold values 0 or 1
- down_mask: int32 [224, 64], P('col', 'row'), may hold values 0 or 1
Outputs:
- output: bfloat16 [512, 8192], P('col', 'row')
- d_tokens: bfloat16 [512, 8192], P('col', 'row')
- grad_gate: bfloat16 [8192, 28672], P('row', 'col')
- grad_up: bfloat16 [8192, 28672], P('row', 'col')
- grad_down: bfloat16 [28672, 8192], P('col', 'row')
Inputs may be any that keep to these rules, and one draw needn't show every extreme that they name: `gate_mask`: 1 keeps a block, 0 prunes it. `up_mask`: 1 keeps a block, 0 prunes it. `down_mask`: 1 keeps a block, 0 prunes it.
All inputs are finite; a program needn't handle non-finite values.
Results may differ from a plain program's by a relative error of at most 0.0049.
Values may be sent and summed in bfloat16 or wider, within the bound.
A program may use at most 256 MiB of HBM per device.

v0:
```python
import jax
import jax.numpy as jnp
from jax import lax
from jax.sharding import PartitionSpec as P


def masked(weight, block_mask):
    block_rows, block_cols = block_mask.shape
    total_rows, total_cols = weight.shape
    shaped = weight.reshape(
        block_rows, total_rows // block_rows, block_cols, total_cols // block_cols
    )
    return (shaped * block_mask.astype(weight.dtype)[:, None, :, None]).reshape(
        total_rows, total_cols
    )


def right_product(left, right):
    return lax.dot_general(
        left, right, (((1,), (1,)), ((), ())), preferred_element_type=jnp.float32
    )


def left_product(left, right):
    return lax.dot_general(
        left, right, (((0,), (0,)), ((), ())), preferred_element_type=jnp.float32
    )


def per_device(
    tokens, cotangent, gate_weight, up_weight, down_weight, gate_mask, up_mask, down_mask
):
    gate_eff = masked(gate_weight, gate_mask)
    up_eff = masked(up_weight, up_mask)
    down_eff = masked(down_weight, down_mask)
    rows_all, cot_all = (
        lax.all_gather(tokens, "col", axis=0, tiled=True),
        lax.all_gather(cotangent, "col", axis=0, tiled=True),
    )
    gate_part = jnp.dot(rows_all, gate_eff, preferred_element_type=jnp.float32)
    up_part = jnp.dot(rows_all, up_eff, preferred_element_type=jnp.float32)
    gate_share, up_share = (
        lax.psum_scatter(gate_part, "row", scatter_dimension=0, tiled=True),
        lax.psum_scatter(up_part, "row", scatter_dimension=0, tiled=True),
    )
    activated_share = gate_share * jax.nn.sigmoid(gate_share)
    hidden_share = (activated_share * up_share).astype(jnp.bfloat16)
    hidden_all = lax.all_gather(hidden_share, "row", axis=0, tiled=True)
    output = lax.psum_scatter(
        jnp.dot(hidden_all, down_eff, preferred_element_type=jnp.float32),
        "col",
        scatter_dimension=0,
        tiled=True,
    ).astype(jnp.bfloat16)
    hidden_part = right_product(cot_all, down_eff)
    hidden_grad = lax.psum_scatter(hidden_part, "row", scatter_dimension=0, tiled=True)
    sigmoid_gate = jax.nn.sigmoid(gate_share)
    activated = gate_share * sigmoid_gate
    gate_grad = (
        hidden_grad * up_share * sigmoid_gate * (1.0 + gate_share * (1.0 - sigmoid_gate))
    ).astype(jnp.bfloat16)
    up_grad = (hidden_grad * activated).astype(jnp.bfloat16)
    gate_grad_all, up_grad_all = (
        lax.all_gather(gate_grad, "row", axis=0, tiled=True),
        lax.all_gather(up_grad, "row", axis=0, tiled=True),
    )
    grad_down = masked(left_product(hidden_all, cot_all), down_mask).astype(jnp.bfloat16)
    grad_gate = masked(left_product(rows_all, gate_grad_all), gate_mask).astype(jnp.bfloat16)
    grad_up = masked(left_product(rows_all, up_grad_all), up_mask).astype(jnp.bfloat16)
    d_tokens = lax.psum_scatter(
        right_product(gate_grad_all, gate_eff) + right_product(up_grad_all, up_eff),
        "col",
        scatter_dimension=0,
        tiled=True,
    ).astype(jnp.bfloat16)
    return (output, d_tokens, grad_gate, grad_up, grad_down)


def solution(mesh):
    in_specs = (
        P("col", "row"),
        P("col", "row"),
        P("row", "col"),
        P("row", "col"),
        P("col", "row"),
        P("row", "col"),
        P("row", "col"),
        P("col", "row"),
    )
    out_specs = (
        P("col", "row"),
        P("col", "row"),
        P("row", "col"),
        P("row", "col"),
        P("col", "row"),
    )
    return jax.shard_map(
        per_device, mesh=mesh, in_specs=in_specs, out_specs=out_specs, check_vma=False
    )
```

profile of v0, /device:TPU:0, one launch (start us, length us, event | category | flops | bytes accessed | tf_op | source)
XLA Modules:
  0.0 701.0 jit_solution(3250287517866491269)
XLA Ops:
  9.6 30.7 %all-gather.10.cloned.1.call-done = bf16[512,1024]{1,0:T(8,128)(2,1)} async-done(((bf16[128,1024]{1,0:T(8,128)(2,1)}), bf16[512,1024]{1,0:T(8,128)(2,1)}) %all-gather.10.cloned.1.call-update) | async-done | bytes 1048592 | tf_op jit(solution)/shard_map/all_gather | solution.py:38
  47.7 16.7 %convolution_bitcast_fusion = f32[512,7168]{0,1:T(8,128)} fusion(bf16[512,1024]{1,0:T(8,128)(2,1)S(1)} %copy-done.1, bf16[7168,1024]{1,0:T(8,128)(2,1)} %param.12, bf16[896,8,8,128]{3,2,1,0:T(8,128)(2,1)} %bitcast.70), kind=kOutput, calls=%fused_computation.9 | convolution fusion | flops 7523532800 | bytes 45088768 | tf_op jit(solution)/shard_map/dot_general | solution.py:19
  64.3 14.3 %copy.45 = f32[512,7168]{1,0:T(8,128)} copy(f32[512,7168]{0,1:T(8,128)} %convolution_bitcast_fusion) | data formatting | bytes 29360128
  79.3 9.5 %mul.92 = bf16[8,128,56,128]{3,2,1,0:T(8,128)(2,1)} broadcast(bf16[8,56]{1,0:T(8,128)(2,1)S(1)} %get-tuple-element.26), dimensions={0,2} | broadcast | bytes 14680960 | tf_op jit(solution)/shard_map/mul | solution.py:13
  88.8 27.6 %convolution_bitcast_fusion.1 = f32[512,7168]{0,1:T(8,128)} fusion(bf16[512,1024]{1,0:T(8,128)(2,1)S(1)} %copy-done, bf16[1024,7168]{1,0:T(8,128)(2,1)} %param.11, bf16[128,8,56,128]{3,2,1,0:T(8,128)(2,1)} %bitcast.72), kind=kOutput, calls=%fused_computation.10 | convolution fusion | flops 7523532800 | bytes 45088768 | tf_op jit(solution)/shard_map/dot_general | solution.py:41
  116.4 14.8 %copy.43 = f32[512,7168]{1,0:T(8,128)} copy(f32[512,7168]{0,1:T(8,128)} %convolution_bitcast_fusion.1) | data formatting | bytes 29360128
  131.8 7.4 %mul.88 = bf16[8,128,56,128]{3,2,1,0:T(8,128)(2,1)} broadcast(bf16[8,56]{1,0:T(8,128)(2,1)S(1)} %get-tuple-element.28), dimensions={0,2} | broadcast | bytes 14680960 | tf_op jit(solution)/shard_map/mul | solution.py:13
  139.3 23.8 %convolution_bitcast_fusion.2 = f32[512,7168]{0,1:T(8,128)} fusion(bf16[512,1024]{1,0:T(8,128)(2,1)S(1)} %copy-done, bf16[1024,7168]{1,0:T(8,128)(2,1)} %param.10, bf16[128,8,56,128]{3,2,1,0:T(8,128)(2,1)} %bitcast.74), kind=kOutput, calls=%fused_computation.11 | convolution fusion | flops 7523532800 | bytes 45088768 | tf_op jit(solution)/shard_map/dot_general | solution.py:40
  163.0 14.3 %copy.41 = f32[512,7168]{1,0:T(8,128)} copy(f32[512,7168]{0,1:T(8,128)} %convolution_bitcast_fusion.2) | data formatting | bytes 29360128
  181.9 106.9 %reduce-scatter.18.cloned.1.call-done = f32[64,7168]{1,0:T(8,128)} async-done(((f32[512,7168]{1,0:T(8,128)}), f32[64,7168]{1,0:T(8,128)}) %reduce-scatter.18.cloned.1.call-update) | async-done | bytes 1835024 | tf_op jit(solution)/shard_map/reduce_scatter | solution.py:44
  288.8 106.9 %reduce-scatter.16.cloned.1.call-done = f32[64,7168]{1,0:T(8,128)} async-done(((f32[512,7168]{1,0:T(8,128)}), f32[64,7168]{1,0:T(8,128)}) %reduce-scatter.16.cloned.1.call-update) | async-done | bytes 1835024 | tf_op jit(solution)/shard_map/reduce_scatter | solution.py:43
  402.6 48.3 %all-gather.12.cloned.1.call-done = bf16[512,7168]{1,0:T(8,128)(2,1)} async-done(((bf16[64,7168]{1,0:T(8,128)(2,1)}), bf16[512,7168]{1,0:T(8,128)(2,1)}) %all-gather.12.cloned.1.call-update) | async-done | bytes 7340048 | tf_op jit(solution)/shard_map/all_gather | solution.py:64
  450.9 16.3 %fusion.3 = f32[512,1024]{1,0:T(8,128)S(1)} fusion(bf16[512,7168]{1,0:T(8,128)(2,1)} %all-gather.12.cloned.1.call-done, bf16[1024,7168]{1,0:T(8,128)(2,1)} %param.10, bf16[128,8,56,128]{3,2,1,0:T(8,128)(2,1)} %bitcast.75), kind=kOutput, calls=%fused_computation.12 | convolution fusion | flops 7523532800 | bytes 38797312 | tf_op jit(solution)/shard_map/dot_general | solution.py:19
  467.3 36.1 %all-gather.14.cloned.1.call-done = bf16[512,7168]{1,0:T(8,128)(2,1)} async-done(((bf16[64,7168]{1,0:T(8,128)(2,1)}), bf16[512,7168]{1,0:T(8,128)(2,1)}) %all-gather.14.cloned.1.call-update) | async-done | bytes 7340048 | tf_op jit(solution)/shard_map/all_gather | solution.py:65
  503.4 17.4 %fusion.7 = f32[512,1024]{1,0:T(8,128)} fusion(f32[512,1024]{1,0:T(8,128)S(1)} %fusion.3, bf16[512,7168]{1,0:T(8,128)(2,1)} %all-gather.14.cloned.1.call-done, bf16[1024,7168]{1,0:T(8,128)(2,1)} %param.11, bf16[128,8,56,128]{3,2,1,0:T(8,128)(2,1)} %bitcast.73), kind=kOutput, calls=%fused_computation.20 | convolution fusion | flops 7524057088 | bytes 40894464 | tf_op jit(solution)/shard_map/dot_general | solution.py:19
  521.1 12.8 %mul.104 = f32[8,128,56,128]{1,0,3,2:T(8,128)} broadcast(f32[8,56]{0,1:T(8,128)S(1)} %copy.36), dimensions={0,2} | broadcast | bytes 29361920 | tf_op jit(solution)/shard_map/mul | solution.py:13
  533.9 23.9 %fusion.2 = bf16[1024,7168]{0,1:T(8,128)(2,1)} fusion(f32[896,8,8,128]{3,2,1,0:T(8,128)} %bitcast.69, bf16[512,7168]{1,0:T(8,128)(2,1)} %all-gather.12.cloned.1.call-done, bf16[512,1024]{1,0:T(8,128)(2,1)S(1)} %copy-done), kind=kOutput, calls=%fused_computation.5 | convolution fusion | flops 7530872832 | bytes 52428800 | tf_op jit(solution)/shard_map/dot_general | solution.py:25
  557.8 20.2 %copy.39 = bf16[1024,7168]{1,0:T(8,128)(2,1)} copy(bf16[1024,7168]{0,1:T(8,128)(2,1)} %fusion.2) | data formatting | bytes 29360128
  578.0 20.7 %fusion.5 = f32[512,1024]{1,0:T(8,128)} fusion(bf16[512,7168]{1,0:T(8,128)(2,1)} %all-gather.8.cloned.1.call-done, bf16[7168,1024]{1,0:T(8,128)(2,1)} %param.12, bf16[896,8,8,128]{3,2,1,0:T(8,128)(2,1)} %bitcast.71), kind=kOutput, calls=%fused_computation.14 | convolution fusion | flops 7523532800 | bytes 38797312 | tf_op jit(solution)/shard_map/dot_general | solution.py:50
  598.7 12.1 %mul.107 = f32[8,128,56,128]{1,0,3,2:T(8,128)} broadcast(f32[8,56]{0,1:T(8,128)S(1)} %copy.37), dimensions={0,2} | broadcast | bytes 29361920 | tf_op jit(solution)/shard_map/mul | solution.py:13
  610.8 24.2 %fusion.1 = bf16[1024,7168]{0,1:T(8,128)(2,1)} fusion(f32[896,8,8,128]{3,2,1,0:T(8,128)} %bitcast.67, bf16[512,7168]{1,0:T(8,128)(2,1)} %all-gather.14.cloned.1.call-done, bf16[512,1024]{1,0:T(8,128)(2,1)S(1)} %copy-done), kind=kOutput, calls=%fused_computation.3 | convolution fusion | flops 7530872832 | bytes 52428800 | tf_op jit(solution)/shard_map/dot_general | solution.py:25
  635.0 19.9 %copy.40 = bf16[1024,7168]{1,0:T(8,128)(2,1)} copy(bf16[1024,7168]{0,1:T(8,128)(2,1)} %fusion.1) | data formatting | bytes 29360128
  654.9 11.6 %mul.110 = f32[56,128,8,128]{3,2,1,0:T(8,128)} broadcast(f32[56,8]{1,0:T(8,128)S(1)} %copy.38), dimensions={0,2} | broadcast | bytes 29361920 | tf_op jit(solution)/shard_map/mul | solution.py:13
  666.6 23.8 %fusion = bf16[7168,1024]{1,0:T(8,128)(2,1)} fusion(f32[896,8,8,128]{3,2,1,0:T(8,128)} %bitcast.68, bf16[512,7168]{1,0:T(8,128)(2,1)} %all-gather.8.cloned.1.call-done, bf16[512,1024]{1,0:T(8,128)(2,1)S(1)} %copy-done.2), kind=kOutput, calls=%fused_computation.1 | convolution fusion | flops 7530872832 | bytes 52428800 | tf_op jit(solution)/shard_map/dot_general | solution.py:25
  (46 shorter events, 26.4 us)
Async XLA Ops:
  7.2 33.1 %all-gather.10.cloned.1.call-start = ((), (), s32[]{:S(2)}) async-start(), calls=%async_computation.8 | async-start | bytes 1310720 | tf_op jit(solution)/shard_map/all_gather | solution.py:38
  7.9 71.4 %all-gather.6.cloned.1.call-start = ((), (), s32[]{:S(2)}) async-start(), calls=%async_computation.5 | async-start | bytes 1310720 | tf_op jit(solution)/shard_map/all_gather | solution.py:37
  8.6 173.3 %reduce-scatter.20.cloned.1.call-start = ((), (), s32[]{:S(2)}) async-start(), calls=%async_computation.14 | async-start | bytes 16515072 | tf_op jit(solution)/shard_map/reduce_scatter | solution.py:56
  40.2 7.4 %copy-start.1 = (bf16[512,1024]{1,0:T(8,128)(2,1)S(1)}, bf16[512,1024]{1,0:T(8,128)(2,1)}, u32[]{:S(2)}) copy-start(bf16[512,1024]{1,0:T(8,128)(2,1)} %all-gather.10.cloned.1.call-done) | copy-start | bytes 3145732
  78.6 0.7 copy-start.3
  78.6 210.2 %reduce-scatter.18.cloned.1.call-start = ((), (), s32[]{:S(2)}) async-start(), calls=%async_computation.13 | async-start | bytes 16515072 | tf_op jit(solution)/shard_map/reduce_scatter | solution.py:44
  79.3 9.5 %copy-start = (bf16[512,1024]{1,0:T(8,128)(2,1)S(1)}, bf16[512,1024]{1,0:T(8,128)(2,1)}, u32[]{:S(2)}) copy-start(bf16[512,1024]{1,0:T(8,128)(2,1)} %all-gather.6.cloned.1.call-done) | copy-start | bytes 3145732
  131.1 0.7 copy-start.4
  131.2 264.5 %reduce-scatter.16.cloned.1.call-start = ((), (), s32[]{:S(2)}) async-start(), calls=%async_computation.12 | async-start | bytes 16515072 | tf_op jit(solution)/shard_map/reduce_scatter | solution.py:43
  177.4 273.5 %all-gather.12.cloned.1.call-start = ((), (), s32[]{:S(2)}) async-start(), calls=%async_computation.9 | async-start | bytes 8257536 | tf_op jit(solution)/shard_map/all_gather | solution.py:64
  400.8 102.5 %all-gather.14.cloned.1.call-start = ((), (), s32[]{:S(2)}) async-start(), calls=%async_computation.10 | async-start | bytes 8257536 | tf_op jit(solution)/shard_map/all_gather | solution.py:65
  401.6 176.4 %all-gather.8.cloned.1.call-start = ((), (), s32[]{:S(2)}) async-start(), calls=%async_computation.6 | async-start | bytes 8257536 | tf_op jit(solution)/shard_map/all_gather | solution.py:48
  402.3 288.1 %reduce-scatter.14.cloned.1.call-start = ((), (), s32[]{:S(2)}) async-start(), calls=%async_computation.11 | async-start | bytes 2621440 | tf_op jit(solution)/shard_map/reduce_scatter | solution.py:70
  520.8 171.4 %reduce-scatter.12.cloned.1.call-start = ((), (), s32[]{:S(2)}) async-start(), calls=%async_computation.7 | async-start | bytes 2621440 | tf_op jit(solution)/shard_map/reduce_scatter | solution.py:49
  654.9 11.6 %copy-start.2 = (bf16[512,1024]{1,0:T(8,128)(2,1)S(1)}, bf16[512,1024]{1,0:T(8,128)(2,1)}, u32[]{:S(2)}) copy-start(bf16[512,1024]{1,0:T(8,128)(2,1)} %all-gather.10.cloned.1.call-done) | copy-start | bytes 3145732
Sparse Core Ops, SparseCore 0:
  9.6 30.6 all-gather.9
  41.8 27.4 all-gather.5
  78.7 103.1 reduce-scatter.19
  185.3 103.5 reduce-scatter.17
  292.2 103.5 reduce-scatter.15
  400.9 49.9 all-gather.11
  453.4 49.9 all-gather.13
  505.3 49.9 all-gather.7
  557.5 43.8 reduce-scatter.13
  603.7 43.1 reduce-scatter.11
where the time goes:
time: 708 us; the launch traced here: 701 us
  waiting for transfers between devices  336 us (47%)
  matrix products  194 us (27%)
  local copies, waits for them, and re-layouts  145 us (20%)
  between operations  14.4 us (2%)
  other arithmetic  9.42 us (1%)
    reduce_scatter x1, waiting for transfers between devices, per_device(): lax.psum_scatter(up_part, 'row', scatter_dimension=0, tiled=True)  107 us
    reduce_scatter x1, waiting for transfers between devices, per_device(): lax.psum_scatter(gate_part, 'row', scatter_dimension=0, tiled=True)  107 us
    unnamed x15, local copies, waits for them, and re-layouts  83.9 us
    dot_general x3, matrix products, left_product(): lax.dot_general(left, right, (((0,), (0,)), ((), ())), preferred_element_...  71.9 us
    mul x6, local copies, waits for them, and re-layouts, masked(): shaped * block_mask.astype(weight.dtype)[:, None, :, None]  60.9 us
    dot_general x3, matrix products, right_product(): lax.dot_general(left, right, (((1,), (1,)), ((), ())), preferred_element_...  50.4 us
    all_gather x1, waiting for transfers between devices, per_device(): lax.all_gather(gate_grad, 'row', axis=0, tiled=True)  48.3 us
    all_gather x1, waiting for transfers between devices, per_device(): lax.all_gather(up_grad, 'row', axis=0, tiled=True)  36.1 us
  transfers between devices with their start and end apart: 10, of which 6 were waited for; matrix products, arithmetic and copies ran while one was open for 49% of the time, Pallas kernels for 0%

commit v1 on v0

v1 whole, which is shorter than its diff:
```python
import functools

import jax
import jax.numpy as jnp
from jax import lax
from jax.experimental import pallas as pl
from jax.experimental.pallas import tpu as pltpu
from jax.sharding import PartitionSpec as P

BLK = 128
F32 = jnp.float32
BF16 = jnp.bfloat16
LIMIT = 48 * 1024 * 1024


def tile_of(width):
    for tile in (512, 256, 128):
        if width % tile == 0:
            return tile
    return width


def params():
    return pltpu.CompilerParams(
        vmem_limit_bytes=LIMIT
    )


def cost(*arrays, flops):
    moved = sum(a.size * jnp.dtype(a.dtype).itemsize for a in arrays)
    return pl.CostEstimate(flops=flops, bytes_accessed=moved, transcendentals=0)


def keep_blocks(value, mask_ref, row0, col0):
    rows, cols = value.shape
    strips = []
    for i in range(rows // BLK):
        pieces = []
        for j in range(cols // BLK):
            keep = mask_ref[row0 + i, col0 + j].astype(F32)
            piece = value[i * BLK : (i + 1) * BLK, j * BLK : (j + 1) * BLK]
            pieces.append(piece * jnp.full((BLK, BLK), keep, F32).astype(value.dtype))
        strips.append(jnp.concatenate(pieces, axis=1))
    return jnp.concatenate(strips, axis=0)


def dot(a, b, dims):
    return lax.dot_general(a, b, (dims, ((), ())), preferred_element_type=F32)


NN = ((1,), (0,))
NT = ((1,), (1,))
TN = ((0,), (0,))

SMEM = functools.partial(pl.BlockSpec, memory_space=pltpu.SMEM)


def gate_up_kernel(first, wide, gm_ref, um_ref, x_ref, g_ref, u_ref, keep_ref, send_ref):
    half = x_ref.shape[0] // 2
    col0 = (first + pl.program_id(0)) * wide
    for slot, (m_ref, w_ref) in enumerate(((gm_ref, g_ref), (um_ref, u_ref))):
        part = dot(x_ref[...], keep_blocks(w_ref[...], m_ref, 0, col0), NN)
        keep_ref[slot] = part[:half]
        send_ref[slot] = part[half:]


def gate_up(x, gate, up, gm, um, start, width):
    tokens, depth = x.shape
    tile = tile_of(width)
    first = start // tile
    weight = pl.BlockSpec((depth, tile), lambda i: (0, first + i))
    out = jax.ShapeDtypeStruct((2, tokens // 2, width), F32)
    return pl.pallas_call(
        functools.partial(gate_up_kernel, first, tile // BLK),
        grid=(width // tile,),
        in_specs=[SMEM(), SMEM(), pl.BlockSpec((tokens, depth), lambda i: (0, 0)), weight, weight],
        out_specs=[pl.BlockSpec((2, tokens // 2, tile), lambda i: (0, 0, i))] * 2,
        out_shape=[out, out],
        compiler_params=params(),
        cost_estimate=cost(x, out, out, out, flops=4 * tokens * depth * width),
        name="gate_up",
    )(gm, um, x, gate, up)


def d_hidden_kernel(first, tall, m_ref, x_ref, w_ref, keep_ref, send_ref):
    half = x_ref.shape[0] // 2
    row0 = (first + pl.program_id(0)) * tall
    part = dot(x_ref[...], keep_blocks(w_ref[...], m_ref, row0, 0), NT)
    keep_ref[0] = part[:half]
    send_ref[0] = part[half:]


def d_hidden(x, down, dm, start, width):
    tokens, depth = x.shape
    tile = tile_of(width)
    first = start // tile
    out = jax.ShapeDtypeStruct((1, tokens // 2, width), F32)
    return pl.pallas_call(
        functools.partial(d_hidden_kernel, first, tile // BLK),
        grid=(width // tile,),
        in_specs=[
            SMEM(),
            pl.BlockSpec((tokens, depth), lambda i: (0, 0)),
            pl.BlockSpec((tile, depth), lambda i: (first + i, 0)),
        ],
        out_specs=[pl.BlockSpec((1, tokens // 2, tile), lambda i: (0, 0, i))] * 2,
        out_shape=[out, out],
        compiler_params=params(),
        cost_estimate=cost(x, out, out, flops=2 * tokens * depth * width),
        name="d_hidden",
    )(dm, x, down)


def halves_specs(groups, half, tile, steps):
    low = pl.BlockSpec((groups, half, tile), lambda i: (0, 0, jnp.minimum(i, steps - 1)))
    high = pl.BlockSpec((groups, half, tile), lambda i: (0, 0, jnp.maximum(i - steps, 0)))
    return [low, low, high, high]


def pick(steps, refs, slot, low):
    a, b = (refs[0], refs[1]) if low else (refs[2], refs[3])
    return jnp.concatenate([a[slot], b[slot]], axis=0)


def both(steps, body):
    i = pl.program_id(0)

    @pl.when(i < steps)
    def _():
        body(True)

    @pl.when(i >= steps)
    def _():
        body(False)


def down_kernel(steps, tall, m_ref, c_ref, w_ref, *rest):
    refs, (out_ref, grad_ref) = rest[:4], rest[4:]
    i = pl.program_id(0)

    @pl.when(i == 0)
    def _():
        out_ref[...] = jnp.zeros_like(out_ref)

    def body(low):
        hid = pick(steps, refs, 0, low)
        out_ref[...] += dot(hid, keep_blocks(w_ref[...], m_ref, i * tall, 0), NN)
        grad = dot(hid, c_ref[...], TN)
        grad_ref[...] = keep_blocks(grad, m_ref, i * tall, 0).astype(BF16)

    both(steps, body)


def down_side(cot, down, dm, pieces):
    tokens, depth = cot.shape
    hid = down.shape[0]
    width = hid // 2
    tile = tile_of(width)
    steps = width // tile
    rows = pl.BlockSpec((tile, depth), lambda i: (i, 0))
    return pl.pallas_call(
        functools.partial(down_kernel, steps, tile // BLK),
        grid=(2 * steps,),
        in_specs=[SMEM(), pl.BlockSpec((tokens, depth), lambda i: (0, 0)), rows]
        + halves_specs(1, tokens // 2, tile, steps),
        out_specs=[pl.BlockSpec((tokens, depth), lambda i: (0, 0)), rows],
        out_shape=[
            jax.ShapeDtypeStruct((tokens, depth), F32),
            jax.ShapeDtypeStruct((hid, depth), BF16),
        ],
        compiler_params=params(),
        cost_estimate=cost(cot, down, down, *pieces, flops=4 * tokens * depth * hid),
        name="down_side",
    )(dm, cot, down, *pieces)


def d_tokens_kernel(steps, wide, gm_ref, um_ref, g_ref, u_ref, *rest):
    refs, out_ref = rest[:4], rest[4]
    i = pl.program_id(0)

    @pl.when(i == 0)
    def _():
        out_ref[...] = jnp.zeros_like(out_ref)

    def body(low):
        out_ref[...] += dot(
            pick(steps, refs, 0, low), keep_blocks(g_ref[...], gm_ref, 0, i * wide), NT
        ) + dot(pick(steps, refs, 1, low), keep_blocks(u_ref[...], um_ref, 0, i * wide), NT)

    both(steps, body)


def d_tokens_part(gate, up, gm, um, pieces):
    depth, hid = gate.shape
    tokens = 2 * pieces[0].shape[1]
    width = hid // 2
    tile = tile_of(width)
    steps = width // tile
    weight = pl.BlockSpec((depth, tile), lambda i: (0, i))
    return pl.pallas_call(
        functools.partial(d_tokens_kernel, steps, tile // BLK),
        grid=(2 * steps,),
        in_specs=[SMEM(), SMEM(), weight, weight] + halves_specs(2, tokens // 2, tile, steps),
        out_specs=pl.BlockSpec((tokens, depth), lambda i: (0, 0)),
        out_shape=jax.ShapeDtypeStruct((tokens, depth), F32),
        compiler_params=params(),
        cost_estimate=cost(gate, up, *pieces, flops=4 * tokens * depth * hid),
        name="d_tokens",
    )(gm, um, gate, up, *pieces)


def grads_kernel(steps, wide, gm_ref, um_ref, xt_ref, *rest):
    refs, outs = rest[:4], rest[4:]
    i = pl.program_id(0)

    def body(low):
        for slot, (m_ref, out_ref) in enumerate(zip((gm_ref, um_ref), outs)):
            grad = dot(xt_ref[...], pick(steps, refs, slot, low), NN)
            out_ref[...] = keep_blocks(grad, m_ref, 0, i * wide).astype(BF16)

    both(steps, body)


def weight_grads(xt, gm, um, pieces):
    depth, tokens = xt.shape
    width = pieces[0].shape[2]
    tile = tile_of(width)
    steps = width // tile
    out = jax.ShapeDtypeStruct((depth, 2 * width), BF16)
    return pl.pallas_call(
        functools.partial(grads_kernel, steps, tile // BLK),
        grid=(2 * steps,),
        in_specs=[SMEM(), SMEM(), pl.BlockSpec((depth, tokens), lambda i: (0, 0))]
        + halves_specs(2, tokens // 2, tile, steps),
        out_specs=[pl.BlockSpec((depth, tile), lambda i: (0, i))] * 2,
        out_shape=[out, out],
        compiler_params=params(),
        cost_estimate=cost(out, out, *pieces, flops=8 * tokens * depth * width),
        name="weight_grads",
    )(gm, um, xt, *pieces)


def move_kernel(index_ref, from_ref, to_ref):
    to_ref[...] = from_ref[...]


def ordered(value, index):
    count, width = index.shape[0], value.shape[1]
    block = value.shape[0] // count
    return pl.pallas_call(
        move_kernel,
        grid_spec=pltpu.PrefetchScalarGridSpec(
            num_scalar_prefetch=1,
            grid=(count,),
            in_specs=[pl.BlockSpec((block, width), lambda i, index: (index[i], 0))],
            out_specs=pl.BlockSpec((block, width), lambda i, index: (i, 0)),
        ),
        out_shape=jax.ShapeDtypeStruct(value.shape, value.dtype),
        compiler_params=params(),
        cost_estimate=cost(value, value, flops=0),
        name="ordered",
    )(index, value)


def swap(value, bit, rows):
    return lax.ppermute(value, "row", [(i, i ^ bit) for i in range(rows)])


def reduce_rows(keep, send, order, rows):
    groups, half, width = keep.shape
    total = keep + swap(send, 1, rows)
    left = sorted(order, reverse=True)
    total = total.reshape((groups,) + (2,) * len(left) + (half * 2 // rows, width))
    for bit in order:
        axis = 1 + left.index(bit)
        away = lax.index_in_dim(total, 1, axis, keepdims=False).astype(BF16)
        stay = lax.index_in_dim(total, 0, axis, keepdims=False)
        total = stay + swap(away, bit, rows).astype(F32)
        left.remove(bit)
    return total


def gather_rows(share, order, rows):
    groups, block, width = share.shape
    have = []
    value = share
    for bit in reversed(order):
        have = sorted(have + [bit], reverse=True)
        value = jnp.stack([value, swap(value, bit, rows)], axis=1 + have.index(bit))
    value = value.reshape(groups, block * rows // 2, width)
    return value, swap(value, 1, rows)


def per_device(
    tokens, cotangent, gate_weight, up_weight, down_weight, gate_mask, up_mask, down_mask
):
    rows = lax.axis_size("row")
    me = lax.axis_index("row")
    hid = down_weight.shape[0]
    width = hid // 2
    bits = [1 << b for b in range(1, rows.bit_length() - 1)]
    orders = (bits, bits[::-1])

    place = jnp.arange(rows)
    half_rows = rows // 2
    relative = ((place % half_rows) * 2 + place // half_rows) ^ me
    other = place ^ me
    back = (other % 2) * half_rows + other // 2

    cot = ordered(lax.all_gather(cotangent, "col", axis=0, tiled=True), relative)
    x = ordered(lax.all_gather(tokens, "col", axis=0, tiled=True), relative)
    xt = x.T

    d_hid = []
    for k, order in enumerate(orders):
        keep, send = d_hidden(cot, down_weight, down_mask, k * width, width)
        d_hid.append(reduce_rows(keep, send, order, rows)[0])
    hidden_pieces, grad_pieces = [], []
    shares = []
    for k, order in enumerate(orders):
        keep, send = gate_up(
            x, gate_weight, up_weight, gate_mask, up_mask, k * width, width
        )
        shares.append(reduce_rows(keep, send, order, rows))
    for k, order in enumerate(orders):
        gate, up = shares[k][0], shares[k][1]
        hidden = (gate * jax.nn.sigmoid(gate) * up).astype(BF16)
        hidden_pieces += gather_rows(hidden[None], order, rows)
    for k, order in enumerate(orders):
        gate, up, dh = shares[k][0], shares[k][1], d_hid[k]
        s = jax.nn.sigmoid(gate)
        d_gate = (dh * up * s * (1.0 + gate * (1.0 - s))).astype(BF16)
        d_up = (dh * (gate * s)).astype(BF16)
        grad_pieces += gather_rows(jnp.stack([d_gate, d_up]), order, rows)

    def spread(part):
        return lax.psum_scatter(
            ordered(part, back), "col", scatter_dimension=0, tiled=True
        ).astype(BF16)

    part, grad_down = down_side(cot, down_weight, down_mask, hidden_pieces)
    output = spread(part)
    d_tokens = spread(d_tokens_part(gate_weight, up_weight, gate_mask, up_mask, grad_pieces))
    grad_gate, grad_up = weight_grads(xt, gate_mask, up_mask, grad_pieces)
    return (output, d_tokens, grad_gate, grad_up, grad_down)


def solution(mesh):
    model, weight, down = P("col", "row"), P("row", "col"), P("col", "row")
    return jax.shard_map(
        per_device,
        mesh=mesh,
        in_specs=(model, model, weight, weight, down, weight, weight, down),
        out_specs=(model, model, weight, weight, down),
        check_vma=False,
    )
```

time: 708 us -> 443 us (0.63)
  matrix products: 194 us -> 0 us
  Pallas kernels: 0 us -> 133 us
  local copies, waits for them, and re-layouts: 145 us -> 20.5 us
  waiting for transfers between devices: 336 us -> 219 us
  other arithmetic: 9.42 us -> 33.4 us
  starting transfers between devices: 1.6 us -> 21 us
    dot_general x9 -> x0, matrix products: 194 us -> none  [the longest x3 71.9 us: left_product(): lax.dot_general(left, right, (((0,), (0,)), ((), ())), preferred_element_...]
    reduce_scatter x5 -> x2, waiting for transfers between devices: 218 us -> 32.8 us  [spread(): lax.psum_scatter(ordered(part, back), 'col', scatter_dimension=0, tiled=T...]
    ppermute x0 -> x24, waiting for transfers between devices: none -> 151 us  [swap(): return lax.ppermute(value, 'row', [(i, i ^ bit) for i in range(rows)])]
    pallas_call x0 -> x11, Pallas kernels: none -> 133 us  [the longest x2 30.9 us: gate_up(): pl.pallas_call(functools.partial(gate_up_kernel, first, tile // BLK), gri...]
    all_gather x4 -> x1, waiting for transfers between devices: 84.4 us -> 3.59 us  [per_device(): x = ordered(lax.all_gather(tokens, 'col', axis=0, tiled=True), relative)]
    unnamed x15 -> x33, local copies, waits for them, and re-layouts: 83.9 us -> 12.7 us
    mul x6 -> x0, local copies, waits for them, and re-layouts: 60.9 us -> none  [masked(): shaped * block_mask.astype(weight.dtype)[:, None, :, None]]
    add x0 -> x11, other arithmetic: none -> 24.4 us  [the longest x4 21.2 us: reduce_rows(): total = keep + swap(send, 1, rows)]
  transfers between devices with their start and end apart: 10 -> 28, of which waited for: 6 -> 13; matrix products, arithmetic and copies ran while one was open for 49% -> 9% of each run, Pallas kernels for 0% -> 30%
where the time goes in v1:
time: 443 us; the launch traced here: 441 us
  waiting for transfers between devices  219 us (49%)
  Pallas kernels  133 us (30%)
  other arithmetic  33.4 us (8%)
  starting transfers between devices  21 us (5%)
  local copies, waits for them, and re-layouts  20.5 us (5%)
  between operations  14.2 us (3%)
    ppermute x24, waiting for transfers between devices, swap(): return lax.ppermute(value, 'row', [(i, i ^ bit) for i in range(rows)])  151 us
    reduce_scatter x2, waiting for transfers between devices, spread(): lax.psum_scatter(ordered(part, back), 'col', scatter_dimension=0, tiled=T...  32.8 us
    pallas_call x2, Pallas kernels, gate_up(): pl.pallas_call(functools.partial(gate_up_kernel, first, tile // BLK), gri...  30.9 us
    all_gather x1, waiting for transfers between devices, per_device(): lax.all_gather(cotangent, 'col', axis=0, tiled=True)  30.8 us
    pallas_call x1, Pallas kernels, weight_grads(): pl.pallas_call(functools.partial(grads_kernel, steps, tile // BLK), grid=...  25.3 us
    pallas_call x1, Pallas kernels, d_tokens_part(): pl.pallas_call(functools.partial(d_tokens_kernel, steps, tile // BLK), gr...  24.7 us
    pallas_call x1, Pallas kernels, down_side(): pl.pallas_call(functools.partial(down_kernel, steps, tile // BLK), grid=(...  24.1 us
    add x4, other arithmetic, reduce_rows(): total = keep + swap(send, 1, rows)  21.2 us
  transfers between devices with their start and end apart: 28, of which 13 were waited for; matrix products, arithmetic and copies ran while one was open for 9% of the time, Pallas kernels for 30%

profile of v1, /device:TPU:0, one launch (start us, length us, event | category | flops | bytes accessed | tf_op | source)
XLA Modules:
  0.0 441.1 jit_solution(13454434825069785140)
XLA Ops:
  9.5 30.8 %all-gather.3.cloned.1.call-done.from_ref = bf16[512,1024]{1,0:T(8,128)(2,1)} async-done(((bf16[128,1024]{1,0:T(8,128)(2,1)}), bf16[512,1024]{1,0:T(8,128)(2,1)}) %all-gather.3.cloned.1.call-update) | async-done | bytes 1048592 | tf_op jit(solution)/shard_map/all_gather | solution.py:310
  42.2 9.6 %d_hidden.3 = (f32[1,256,3584]{2,1,0:T(8,128)S(1)}, f32[1,256,3584]{2,1,0:T(8,128)}) custom-call(s32[56,8]{1,0:T(8,128)S(1)} %copy.18.m_ref, bf16[512,1024]{1,0:T(8,128)(2,1)S(1)} %ordered.4.c_ref.x_ref, bf16[7168,1024]{1,0:T(8,128)(2,1)} %w_ref.5), custom_call_target="tpu_custom_call" | custom-call | flops 3758096384 | bytes 8388608 | tf_op jit(solution)/shard_map/d_hidden/pallas_call | solution.py:98
  53.7 9.6 %d_hidden.2 = (f32[1,256,3584]{2,1,0:T(8,128)S(1)}, f32[1,256,3584]{2,1,0:T(8,128)}) custom-call(s32[56,8]{1,0:T(8,128)S(1)} %copy.18.m_ref, bf16[512,1024]{1,0:T(8,128)(2,1)S(1)} %ordered.4.c_ref.x_ref, bf16[7168,1024]{1,0:T(8,128)(2,1)} %w_ref.5), custom_call_target="tpu_custom_call" | custom-call | flops 3758096384 | bytes 8388608 | tf_op jit(solution)/shard_map/d_hidden/pallas_call | solution.py:98
  65.7 3.6 all-gather.5.cloned.1.call-done.from_ref
  71.3 15.4 %gate_up.3 = (f32[2,256,3584]{2,1,0:T(8,128)}, f32[2,256,3584]{2,1,0:T(8,128)}) custom-call(s32[8,56]{1,0:T(8,128)S(1)} %copy-done.7, s32[8,56]{1,0:T(8,128)S(1)} %copy-done.8, bf16[512,1024]{1,0:T(8,128)(2,1)S(1)} %ordered.5.x_ref, bf16[1024,7168]{1,0:T(8,128)(2,1)} %g_ref.5, bf16[1024,7168]{1,0:T(8,128)(2,1)} %u_ref.5), custom_call_target="tpu_custom_call" | custom-call | flops 7516192768 | bytes 23068672 | tf_op jit(solution)/shard_map/gate_up/pallas_call | solution.py:73
  86.7 15.5 %gate_up.2 = (f32[2,256,3584]{2,1,0:T(8,128)}, f32[2,256,3584]{2,1,0:T(8,128)}) custom-call(s32[8,56]{1,0:T(8,128)S(1)} %copy-done.7, s32[8,56]{1,0:T(8,128)S(1)} %copy-done.8, bf16[512,1024]{1,0:T(8,128)(2,1)S(1)} %ordered.5.x_ref, bf16[1024,7168]{1,0:T(8,128)(2,1)} %g_ref.5, bf16[1024,7168]{1,0:T(8,128)(2,1)} %u_ref.5), custom_call_target="tpu_custom_call" | custom-call | flops 7516192768 | bytes 23068672 | tf_op jit(solution)/shard_map/gate_up/pallas_call | solution.py:73
  111.2 16.5 %collective-permute-done.19 = bf16[1,2,64,3584]{3,2,1,0:T(8,128)(2,1)S(1)} collective-permute-done((bf16[1,2,64,3584]{3,2,1,0:T(8,128)(2,1)S(1)}, bf16[1,2,64,3584]{3,2,1,0:T(8,128)(2,1)S(1)}, u32[]{:S(2)}, u32[]{:S(2)}) %collective-permute-start.19) | collective-permute-done | bytes 917536 | tf_op jit(solution)/shard_map/ppermute | solution.py:266
  132.9 3.0 copy-done.9
  135.9 6.5 %add.107 = f32[2,256,3584]{2,1,0:T(8,128)S(1)} add(f32[2,256,3584]{2,1,0:T(8,128)} %get-tuple-element.19, f32[2,256,3584]{2,1,0:T(8,128)} %copy-done.9) | non-fusion elementwise | flops 1835008 | bytes 22020096 | tf_op jit(solution)/shard_map/add | solution.py:271
  145.9 9.5 %add.102 = f32[2,256,3584]{2,1,0:T(8,128)} add(f32[2,256,3584]{2,1,0:T(8,128)} %get-tuple-element.17, f32[2,256,3584]{2,1,0:T(8,128)} %collective-permute-done) | non-fusion elementwise | flops 1835008 | bytes 22020096 | tf_op jit(solution)/shard_map/add | solution.py:271
  159.4 27.7 %collective-permute-done.7 = bf16[2,2,64,3584]{3,2,0,1:T(8,128)(2,1)} collective-permute-done((bf16[2,2,64,3584]{3,2,0,1:T(8,128)(2,1)}, bf16[2,2,64,3584]{3,2,0,1:T(8,128)(2,1)}, u32[]{:S(2)}, u32[]{:S(2)}) %collective-permute-start.7) | collective-permute-done | bytes 1835040 | tf_op jit(solution)/shard_map/ppermute | solution.py:266
  190.6 10.2 %collective-permute-done.1 = bf16[2,2,64,3584]{3,2,0,1:T(8,128)(2,1)S(1)} collective-permute-done((bf16[2,2,64,3584]{3,2,0,1:T(8,128)(2,1)S(1)}, bf16[2,2,64,3584]{3,2,0,1:T(8,128)(2,1)S(1)}, u32[]{:S(2)}, u32[]{:S(2)}) %collective-permute-start.1) | collective-permute-done | bytes 1835040 | tf_op jit(solution)/shard_map/ppermute | solution.py:266
  201.5 15.3 %collective-permute-done.8 = bf16[2,64,3584]{2,1,0:T(8,128)(2,1)S(1)} collective-permute-done((bf16[2,64,3584]{2,1,0:T(8,128)(2,1)S(1)}, bf16[2,64,3584]{2,1,0:T(8,128)(2,1)S(1)}, u32[]{:S(2)}, u32[]{:S(2)}) %collective-permute-start.8) | collective-permute-done | bytes 917536 | tf_op jit(solution)/shard_map/ppermute | solution.py:266
  223.4 23.0 %collective-permute-done.9 = bf16[1,64,3584]{2,1,0:T(8,128)(2,1)S(1)} collective-permute-done((bf16[1,64,3584]{2,1,0:T(8,128)(2,1)S(1)}, bf16[1,64,3584]{2,1,0:T(8,128)(2,1)S(1)}, u32[]{:S(2)}, u32[]{:S(2)}) %collective-permute-start.9) | collective-permute-done | bytes 458784 | tf_op jit(solution)/shard_map/ppermute | solution.py:266
  248.1 5.3 %collective-permute-done.3 = bf16[1,64,3584]{2,1,0:T(8,128)(2,1)S(1)} collective-permute-done((bf16[1,64,3584]{2,1,0:T(8,128)(2,1)S(1)}, bf16[1,64,3584]{2,1,0:T(8,128)(2,1)S(1)}, u32[]{:S(2)}, u32[]{:S(2)}) %collective-permute-start.3) | collective-permute-done | bytes 458784 | tf_op jit(solution)/shard_map/ppermute | solution.py:266
  257.5 15.5 %collective-permute-done.10 = bf16[1,2,64,3584]{3,2,1,0:T(8,128)(2,1)S(1)} collective-permute-done((bf16[1,2,64,3584]{3,2,1,0:T(8,128)(2,1)S(1)}, bf16[1,2,64,3584]{3,2,1,0:T(8,128)(2,1)S(1)}, u32[]{:S(2)}, u32[]{:S(2)}) %collective-permute-start.10) | collective-permute-done | bytes 917536 | tf_op jit(solution)/shard_map/ppermute | solution.py:266
  273.3 3.5 collective-permute-done.4
  277.3 31.0 %collective-permute-done.22 = bf16[2,2,64,3584]{3,2,1,0:T(8,128)(2,1)S(1)} collective-permute-done((bf16[2,2,64,3584]{3,2,1,0:T(8,128)(2,1)S(1)}, bf16[2,2,64,3584]{3,2,1,0:T(8,128)(2,1)S(1)}, u32[]{:S(2)}, u32[]{:S(2)}) %collective-permute-start.22) | collective-permute-done | bytes 1835040 | tf_op jit(solution)/shard_map/ppermute | solution.py:266
  314.6 24.1 %down_side.1 = (f32[512,1024]{1,0:T(8,128)}, bf16[7168,1024]{1,0:T(8,128)(2,1)}) custom-call(s32[56,8]{1,0:T(8,128)S(1)} %copy.18.m_ref, bf16[512,1024]{1,0:T(8,128)(2,1)S(1)} %ordered.4.c_ref.x_ref, bf16[7168,1024]{1,0:T(8,128)(2,1)} %w_ref.5, bf16[1,256,3584]{2,1,0:T(8,128)(2,1)S(1)} %bitcast.124, ...), custom_call_target="tpu_custom_call" | custom-call | flops 15032385536 | bytes 37748736 | tf_op jit(solution)/shard_map/down_side/pallas_call | solution.py:161
  340.3 3.6 ordered.6
  344.0 24.7 %d_tokens.1.from_ref = f32[512,1024]{1,0:T(8,128)S(1)} custom-call(s32[8,56]{1,0:T(8,128)S(1)} %copy-done.7, s32[8,56]{1,0:T(8,128)S(1)} %copy-done.8, bf16[1024,7168]{1,0:T(8,128)(2,1)} %g_ref.5, bf16[1024,7168]{1,0:T(8,128)(2,1)} %u_ref.5, bf16[2,256,3584]{2,1,0:T(8,128)(2,1)} %bitcast.31.rest_0_, bf16[2,256,3584]{2,1,0:T(8,128)(2,1)} %collective-permute-done.17.rest_1_, ...), custom_call_target="tpu_custom_call" | custom-call | flops 15032385536 | bytes 44040192 | tf_op jit(solution)/shard_map/d_tokens/pallas_call | solution.py:200
  368.8 3.6 ordered.7
  372.9 25.3 %weight_grads.1 = (bf16[1024,7168]{1,0:T(8,128)(2,1)}, bf16[1024,7168]{1,0:T(8,128)(2,1)}) custom-call(s32[8,56]{1,0:T(8,128)S(1)} %copy-done.7, s32[8,56]{1,0:T(8,128)S(1)} %copy-done.8, bf16[1024,512]{1,0:T(8,128)(2,1)S(1)} %bitcast.125, bf16[2,256,3584]{2,1,0:T(8,128)(2,1)} %bitcast.31.rest_0_, bf16[2,256,3584]{2,1,0:T(8,128)(2,1)} %collective-permute-done.17.rest_1_, ...), custom_call_target="tpu_custom_call" | custom-call | flops 15032385536 | bytes 44040192 | tf_op jit(solution)/shard_map/weight_grads/pallas_call | solution.py:230
  400.0 32.8 %reduce-scatter.5.cloned.1.call-done = f32[128,1024]{1,0:T(8,128)} async-done(((f32[512,1024]{1,0:T(8,128)}), f32[128,1024]{1,0:T(8,128)}) %reduce-scatter.5.cloned.1.call-update) | async-done | bytes 524304 | tf_op jit(solution)/shard_map/reduce_scatter | solution.py:337
  (120 shorter events, 61.2 us)
Async XLA Ops:
  7.2 33.1 %all-gather.3.cloned.1.call-start = ((), (), s32[]{:S(2)}) async-start(), calls=%async_computation.2 | async-start | bytes 1310720 | tf_op jit(solution)/shard_map/all_gather | solution.py:310
  7.9 61.4 %all-gather.5.cloned.1.call-start = ((), (), s32[]{:S(2)}) async-start(), calls=%async_computation.3 | async-start | bytes 1310720 | tf_op jit(solution)/shard_map/all_gather | solution.py:311
  8.6 389.6 %reduce-scatter.3.cloned.1.call-start = ((), (), s32[]{:S(2)}) async-start(), calls=%async_computation.4 | async-start | bytes 2621440 | tf_op jit(solution)/shard_map/reduce_scatter | solution.py:337
  53.7 49.0 %collective-permute-start.18 = (f32[1,256,3584]{2,1,0:T(8,128)}, f32[1,256,3584]{2,1,0:T(8,128)}, u32[]{:S(2)}, u32[]{:S(2)}) collective-permute-start(f32[1,256,3584]{2,1,0:T(8,128)} %get-tuple-element.25), channel_id=1, source_target_pairs={{0,4},{4,0},{8,12},{12,8},{16,20},{20,16},{24,28},{28,24},{1,5},{5... | collective-permute-start | bytes 11010056 | tf_op jit(solution)/shard_map/ppermute | solution.py:266
  65.2 41.8 %collective-permute-start.12 = (f32[1,256,3584]{2,1,0:T(8,128)}, f32[1,256,3584]{2,1,0:T(8,128)}, u32[]{:S(2)}, u32[]{:S(2)}) collective-permute-start(f32[1,256,3584]{2,1,0:T(8,128)} %get-tuple-element.23), channel_id=1, source_target_pairs={{0,4},{4,0},{8,12},{12,8},{16,20},{20,16},{24,28},{28,24},{1,5},{5... | collective-permute-start | bytes 11010056 | tf_op jit(solution)/shard_map/ppermute | solution.py:266
  86.6 46.2 %collective-permute-start.6 = (f32[2,256,3584]{2,1,0:T(8,128)}, f32[2,256,3584]{2,1,0:T(8,128)S(1)}, u32[]{:S(2)}, u32[]{:S(2)}) collective-permute-start(f32[2,256,3584]{2,1,0:T(8,128)} %get-tuple-element.20), channel_id=1, source_target_pairs={{0,4},{4,0},{8,12},{12,8},{16,20},{20,16},{24,28},{28,24},{1,5},{5... | collective-permute-start | bytes 22020104 | tf_op jit(solution)/shard_map/ppermute | solution.py:266
  102.1 43.8 %collective-permute-start = (f32[2,256,3584]{2,1,0:T(8,128)}, f32[2,256,3584]{2,1,0:T(8,128)}, u32[]{:S(2)}, u32[]{:S(2)}) collective-permute-start(f32[2,256,3584]{2,1,0:T(8,128)} %get-tuple-element.18), channel_id=1, source_target_pairs={{0,4},{4,0},{8,12},{12,8},{16,20},{20,16},{24,28},{28,24},{1,5},{5... | collective-permute-start | bytes 22020104 | tf_op jit(solution)/shard_map/ppermute | solution.py:266
  128.7 88.3 %collective-permute-start.20 = (bf16[1,64,3584]{2,1,0:T(8,128)(2,1)}, bf16[1,64,3584]{2,1,0:T(8,128)(2,1)S(1)}, u32[]{:S(2)}, u32[]{:S(2)}) collective-permute-start(bf16[1,64,3584]{2,1,0:T(8,128)(2,1)} %fusion.25), channel_id=1, source_target_pairs={{0,8},{4,12},{8,0},{12,4},{16,24},{20,28},{24,16},{28,20},{1,9},{5... | collective-permute-start | bytes 1376264 | tf_op jit(solution)/shard_map/ppermute | solution.py:266
  143.8 43.3 %collective-permute-start.7 = (bf16[2,2,64,3584]{3,2,0,1:T(8,128)(2,1)}, bf16[2,2,64,3584]{3,2,0,1:T(8,128)(2,1)}, u32[]{:S(2)}, u32[]{:S(2)}) collective-permute-start(bf16[2,2,64,3584]{3,2,0,1:T(8,128)(2,1)} %fusion.3), channel_id=1, source_target_pairs={{0,16},{4,20},{8,24},{12,28},{16,0},{20,4},{24,8},{28,12},{1,17},{... | collective-permute-start | bytes 5505032 | tf_op jit(solution)/shard_map/ppermute | solution.py:266
  143.8 76.8 %collective-permute-start.14 = (bf16[1,64,3584]{2,1,0:T(8,128)(2,1)S(1)}, bf16[1,64,3584]{2,1,0:T(8,128)(2,1)S(1)}, u32[]{:S(2)}, u32[]{:S(2)}) collective-permute-start(bf16[1,64,3584]{2,1,0:T(8,128)(2,1)S(1)} %fusion.24), channel_id=1, source_target_pairs={{0,16},{4,20},{8,24},{12,28},{16,0},{20,4},{24,8},{28,12},{1,17},{... | collective-permute-start | bytes 1376264 | tf_op jit(solution)/shard_map/ppermute | solution.py:266
  157.8 43.0 %collective-permute-start.1 = (bf16[2,2,64,3584]{3,2,0,1:T(8,128)(2,1)S(1)}, bf16[2,2,64,3584]{3,2,0,1:T(8,128)(2,1)S(1)}, u32[]{:S(2)}, u32[]{:S(2)}) collective-permute-start(bf16[2,2,64,3584]{3,2,0,1:T(8,128)(2,1)S(1)} %fusion.2), channel_id=1, source_target_pairs={{0,8},{4,12},{8,0},{12,4},{16,24},{20,28},{24,16},{28,20},{1,9},{5... | collective-permute-start | bytes 5505032 | tf_op jit(solution)/shard_map/ppermute | solution.py:266
  189.1 27.8 %collective-permute-start.8 = (bf16[2,64,3584]{2,1,0:T(8,128)(2,1)S(1)}, bf16[2,64,3584]{2,1,0:T(8,128)(2,1)S(1)}, u32[]{:S(2)}, u32[]{:S(2)}) collective-permute-start(bf16[2,64,3584]{2,1,0:T(8,128)(2,1)S(1)} %fusion.9), channel_id=1, source_target_pairs={{0,8},{4,12},{8,0},{12,4},{16,24},{20,28},{24,16},{28,20},{1,9},{5... | collective-permute-start | bytes 2752520 | tf_op jit(solution)/shard_map/ppermute | solution.py:266
  217.8 37.4 %collective-permute-start.21 = (bf16[2,64,3584]{2,1,0:T(8,128)(2,1)S(1)}, bf16[2,64,3584]{2,1,0:T(8,128)(2,1)S(1)}, u32[]{:S(2)}, u32[]{:S(2)}) collective-permute-start(bf16[2,64,3584]{2,1,0:T(8,128)(2,1)S(1)} %get-tuple-element.40), channel_id=1, source_target_pairs={{0,8},{4,12},{8,0},{12,4},{16,24},{20,28},{24,16},{28,20},{1,9},{5... | collective-permute-start | bytes 2752520 | tf_op jit(solution)/shard_map/ppermute | solution.py:266
  219.3 27.1 %collective-permute-start.9 = (bf16[1,64,3584]{2,1,0:T(8,128)(2,1)S(1)}, bf16[1,64,3584]{2,1,0:T(8,128)(2,1)S(1)}, u32[]{:S(2)}, u32[]{:S(2)}) collective-permute-start(bf16[1,64,3584]{2,1,0:T(8,128)(2,1)S(1)} %get-tuple-element.35), channel_id=1, source_target_pairs={{0,8},{4,12},{8,0},{12,4},{16,24},{20,28},{24,16},{28,20},{1,9},{5... | collective-permute-start | bytes 1376264 | tf_op jit(solution)/shard_map/ppermute | solution.py:266
  221.3 35.3 %collective-permute-start.15 = (bf16[2,64,3584]{2,1,0:T(8,128)(2,1)S(1)}, bf16[2,64,3584]{2,1,0:T(8,128)(2,1)S(1)}, u32[]{:S(2)}, u32[]{:S(2)}) collective-permute-start(bf16[2,64,3584]{2,1,0:T(8,128)(2,1)S(1)} %get-tuple-element.42), channel_id=1, source_target_pairs={{0,16},{4,20},{8,24},{12,28},{16,0},{20,4},{24,8},{28,12},{1,17},{... | collective-permute-start | bytes 2752520 | tf_op jit(solution)/shard_map/ppermute | solution.py:266
  222.1 31.2 %collective-permute-start.3 = (bf16[1,64,3584]{2,1,0:T(8,128)(2,1)S(1)}, bf16[1,64,3584]{2,1,0:T(8,128)(2,1)S(1)}, u32[]{:S(2)}, u32[]{:S(2)}) collective-permute-start(bf16[1,64,3584]{2,1,0:T(8,128)(2,1)S(1)} %get-tuple-element.38), channel_id=1, source_target_pairs={{0,16},{4,20},{8,24},{12,28},{16,0},{20,4},{24,8},{28,12},{1,17},{... | collective-permute-start | bytes 1376264 | tf_op jit(solution)/shard_map/ppermute | solution.py:266
  246.5 26.5 %collective-permute-start.10 = (bf16[1,2,64,3584]{3,2,1,0:T(8,128)(2,1)S(1)}, bf16[1,2,64,3584]{3,2,1,0:T(8,128)(2,1)S(1)}, u32[]{:S(2)}, u32[]{:S(2)}) collective-permute-start(bf16[1,2,64,3584]{3,2,1,0:T(8,128)(2,1)S(1)} %get-tuple-element.44), channel_id=1, source_target_pairs={{0,16},{4,20},{8,24},{12,28},{16,0},{20,4},{24,8},{28,12},{1,17},{... | collective-permute-start | bytes 2752520 | tf_op jit(solution)/shard_map/ppermute | solution.py:266
  255.4 52.9 %collective-permute-start.22 = (bf16[2,2,64,3584]{3,2,1,0:T(8,128)(2,1)S(1)}, bf16[2,2,64,3584]{3,2,1,0:T(8,128)(2,1)S(1)}, u32[]{:S(2)}, u32[]{:S(2)}) collective-permute-start(bf16[2,2,64,3584]{3,2,1,0:T(8,128)(2,1)S(1)} %get-tuple-element.34), channel_id=1, source_target_pairs={{0,16},{4,20},{8,24},{12,28},{16,0},{20,4},{24,8},{28,12},{1,17},{... | collective-permute-start | bytes 5505032 | tf_op jit(solution)/shard_map/ppermute | solution.py:266
  256.9 53.6 %collective-permute-start.16 = (bf16[2,2,64,3584]{3,2,0,1:T(8,128)(2,1)S(1)}, bf16[2,2,64,3584]{3,2,0,1:T(8,128)(2,1)S(1)}, u32[]{:S(2)}, u32[]{:S(2)}) collective-permute-start(bf16[2,2,64,3584]{3,2,0,1:T(8,128)(2,1)S(1)} %get-tuple-element.37), channel_id=1, source_target_pairs={{0,8},{4,12},{8,0},{12,4},{16,24},{20,28},{24,16},{28,20},{1,9},{5... | collective-permute-start | bytes 5505032 | tf_op jit(solution)/shard_map/ppermute | solution.py:266
  273.2 40.2 %collective-permute-start.11 = (bf16[1,256,3584]{2,1,0:T(8,128)(2,1)S(1)}, bf16[1,256,3584]{2,1,0:T(8,128)(2,1)S(1)}, u32[]{:S(2)}, u32[]{:S(2)}) collective-permute-start(bf16[1,256,3584]{2,1,0:T(8,128)(2,1)S(1)} %bitcast.138), channel_id=1, source_target_pairs={{0,4},{4,0},{8,12},{12,8},{16,20},{20,16},{24,28},{28,24},{1,5},{5... | collective-permute-start | bytes 5505032 | tf_op jit(solution)/shard_map/ppermute | solution.py:266
  277.2 37.4 %collective-permute-start.5 = (bf16[1,256,3584]{2,1,0:T(8,128)(2,1)S(1)}, bf16[1,256,3584]{2,1,0:T(8,128)(2,1)S(1)}, u32[]{:S(2)}, u32[]{:S(2)}) collective-permute-start(bf16[1,256,3584]{2,1,0:T(8,128)(2,1)S(1)} %bitcast.123), channel_id=1, source_target_pairs={{0,4},{4,0},{8,12},{12,8},{16,20},{20,16},{24,28},{28,24},{1,5},{5... | collective-permute-start | bytes 5505032 | tf_op jit(solution)/shard_map/ppermute | solution.py:266
  310.5 33.5 %collective-permute-start.23 = (bf16[2,256,3584]{2,1,0:T(8,128)(2,1)}, bf16[2,256,3584]{2,1,0:T(8,128)(2,1)}, u32[]{:S(2)}, u32[]{:S(2)}) collective-permute-start(bf16[2,256,3584]{2,1,0:T(8,128)(2,1)} %bitcast.43.rest_2_), channel_id=1, source_target_pairs={{0,4},{4,0},{8,12},{12,8},{16,20},{20,16},{24,28},{28,24},{1,5},{5... | collective-permute-start | bytes 11010056 | tf_op jit(solution)/shard_map/ppermute | solution.py:266
  312.9 31.1 %collective-permute-start.17 = (bf16[2,256,3584]{2,1,0:T(8,128)(2,1)}, bf16[2,256,3584]{2,1,0:T(8,128)(2,1)}, u32[]{:S(2)}, u32[]{:S(2)}) collective-permute-start(bf16[2,256,3584]{2,1,0:T(8,128)(2,1)} %bitcast.31.rest_0_), channel_id=1, source_target_pairs={{0,4},{4,0},{8,12},{12,8},{16,20},{20,16},{24,28},{28,24},{1,5},{5... | collective-permute-start | bytes 11010056 | tf_op jit(solution)/shard_map/ppermute | solution.py:266
  343.9 88.9 %reduce-scatter.5.cloned.1.call-start = ((), (), s32[]{:S(2)}) async-start(), calls=%async_computation.5 | async-start | bytes 2621440 | tf_op jit(solution)/shard_map/reduce_scatter | solution.py:337
  (20 other events, 265.2 us)
Sparse Core Ops, SparseCore 0:
  9.6 30.6 all-gather.2
  41.8 27.4 all-gather.4
  344.0 43.2 reduce-scatter.2
  389.6 43.1 reduce-scatter.4

commit v2 on v1

--- a/solution.py
+++ b/solution.py
@@ -266,29 +266,40 @@
     return lax.ppermute(value, "row", [(i, i ^ bit) for i in range(rows)])
 
 
-def reduce_rows(keep, send, order, rows):
+def split(total, bits, bit):
+    axis = 1 + bits.index(bit)
+    away = lax.index_in_dim(total, 1, axis, keepdims=False).astype(BF16)
+    return lax.index_in_dim(total, 0, axis, keepdims=False), away
+
+
+def pair_rows(keep, send, order, rows):
     groups, half, width = keep.shape
     total = keep + swap(send, 1, rows)
-    left = sorted(order, reverse=True)
-    total = total.reshape((groups,) + (2,) * len(left) + (half * 2 // rows, width))
-    for bit in order:
-        axis = 1 + left.index(bit)
-        away = lax.index_in_dim(total, 1, axis, keepdims=False).astype(BF16)
-        stay = lax.index_in_dim(total, 0, axis, keepdims=False)
+    bits = sorted(order, reverse=True)
+    total = total.reshape((groups,) + (2,) * len(bits) + (half * 2 // rows, width))
+    return split(total, bits, order[0])
+
+
+def reduce_rows(stay, away, order, rows):
+    for k, bit in enumerate(order):
         total = stay + swap(away, bit, rows).astype(F32)
-        left.remove(bit)
+        if k + 1 < len(order):
+            stay, away = split(total, sorted(order[k + 1 :], reverse=True), order[k + 1])
     return total
 
 
-def gather_rows(share, order, rows):
+def gather_rows(share, order, rows, tie=None):
     groups, block, width = share.shape
     have = []
     value = share
     for bit in reversed(order):
         have = sorted(have + [bit], reverse=True)
-        value = jnp.stack([value, swap(value, bit, rows)], axis=1 + have.index(bit))
+        other = swap(value, bit, rows)
+        if tie is not None and bit == order[0]:
+            other, tie = lax.optimization_barrier((other, tie))
+        value = jnp.stack([value, other], axis=1 + have.index(bit))
     value = value.reshape(groups, block * rows // 2, width)
-    return value, swap(value, 1, rows)
+    return (value, swap(value, 1, rows)), tie
 
 
 def per_device(
@@ -311,34 +322,42 @@
     x = ordered(lax.all_gather(tokens, "col", axis=0, tiled=True), relative)
     xt = x.T
 
-    d_hid = []
+    stays, aways = [], []
     for k, order in enumerate(orders):
         keep, send = d_hidden(cot, down_weight, down_mask, k * width, width)
-        d_hid.append(reduce_rows(keep, send, order, rows)[0])
+        stay, away = pair_rows(keep, send, order, rows)
+        stays.append(stay)
+        aways.append(away)
+    x, aways = lax.optimization_barrier((x, aways))
+    d_hid = [
+        reduce_rows(stay, away, order, rows)[0]
+        for stay, away, order in zip(stays, aways, orders)
+    ]
     hidden_pieces, grad_pieces = [], []
     shares = []
     for k, order in enumerate(orders):
         keep, send = gate_up(
             x, gate_weight, up_weight, gate_mask, up_mask, k * width, width
         )
-        shares.append(reduce_rows(keep, send, order, rows))
+        shares.append(reduce_rows(*pair_rows(keep, send, order, rows), order, rows))
     for k, order in enumerate(orders):
         gate, up = shares[k][0], shares[k][1]
         hidden = (gate * jax.nn.sigmoid(gate) * up).astype(BF16)
-        hidden_pieces += gather_rows(hidden[None], order, rows)
+        hidden_pieces += gather_rows(hidden[None], order, rows)[0]
+    part, grad_down = down_side(cot, down_weight, down_mask, hidden_pieces)
     for k, order in enumerate(orders):
         gate, up, dh = shares[k][0], shares[k][1], d_hid[k]
         s = jax.nn.sigmoid(gate)
         d_gate = (dh * up * s * (1.0 + gate * (1.0 - s))).astype(BF16)
         d_up = (dh * (gate * s)).astype(BF16)
-        grad_pieces += gather_rows(jnp.stack([d_gate, d_up]), order, rows)
+        pieces, part = gather_rows(jnp.stack([d_gate, d_up]), order, rows, part)
+        grad_pieces += pieces
 
     def spread(part):
         return lax.psum_scatter(
             ordered(part, back), "col", scatter_dimension=0, tiled=True
         ).astype(BF16)
 
-    part, grad_down = down_side(cot, down_weight, down_mask, hidden_pieces)
     output = spread(part)
     d_tokens = spread(d_tokens_part(gate_weight, up_weight, gate_mask, up_mask, grad_pieces))
     grad_gate, grad_up = weight_grads(xt, gate_mask, up_mask, grad_pieces)

time: 443 us -> 454 us (1.025)
  waiting for transfers between devices: 219 us -> 227 us
  other arithmetic: 33.4 us -> 38.5 us
    all_gather x1, waiting for transfers between devices: 3.59 us -> 27.5 us  [per_device(): x = ordered(lax.all_gather(tokens, 'col', axis=0, tiled=True), relative)]
    ppermute x24, waiting for transfers between devices: 151 us -> 141 us  [swap(): return lax.ppermute(value, 'row', [(i, i ^ bit) for i in range(rows)])]
    reduce_scatter x2, waiting for transfers between devices: 32.8 us -> 25.5 us  [spread(): lax.psum_scatter(ordered(part, back), 'col', scatter_dimension=0, tiled=T...]
    unnamed x33 -> x27, local copies, waits for them, and re-layouts: 12.7 us -> 8.46 us
  transfers between devices with their start and end apart: 28 -> 28, of which waited for: 13 -> 17; matrix products, arithmetic and copies ran while one was open for 9% -> 9% of each run, Pallas kernels for 30% -> 24%
where the time goes in v2:
time: 454 us; the launch traced here: 452 us
  waiting for transfers between devices  227 us (50%)
  Pallas kernels  133 us (29%)
  other arithmetic  38.5 us (8%)
  starting transfers between devices  22.6 us (5%)
  local copies, waits for them, and re-layouts  17.4 us (4%)
  between operations  14.1 us (3%)
    ppermute x24, waiting for transfers between devices, swap(): return lax.ppermute(value, 'row', [(i, i ^ bit) for i in range(rows)])  141 us
    all_gather x1, waiting for transfers between devices, per_device(): lax.all_gather(cotangent, 'col', axis=0, tiled=True)  31.5 us
    pallas_call x2, Pallas kernels, gate_up(): pl.pallas_call(functools.partial(gate_up_kernel, first, tile // BLK), gri...  30.8 us
    all_gather x1, waiting for transfers between devices, per_device(): x = ordered(lax.all_gather(tokens, 'col', axis=0, tiled=True), relative)  27.5 us
    reduce_scatter x2, waiting for transfers between devices, spread(): lax.psum_scatter(ordered(part, back), 'col', scatter_dimension=0, tiled=T...  25.5 us
    pallas_call x1, Pallas kernels, weight_grads(): pl.pallas_call(functools.partial(grads_kernel, steps, tile // BLK), grid=...  25.3 us
    pallas_call x1, Pallas kernels, d_tokens_part(): pl.pallas_call(functools.partial(d_tokens_kernel, steps, tile // BLK), gr...  24.9 us
    pallas_call x1, Pallas kernels, down_side(): pl.pallas_call(functools.partial(down_kernel, steps, tile // BLK), grid=(...  24.1 us
  transfers between devices with their start and end apart: 28, of which 17 were waited for; matrix products, arithmetic and copies ran while one was open for 9% of the time, Pallas kernels for 24%

profile of v2, /device:TPU:0, one launch (start us, length us, event | category | flops | bytes accessed | tf_op | source)
XLA Modules:
  0.0 451.9 jit_solution(7818356753969546078)
XLA Ops:
  8.7 31.5 %all-gather.3.cloned.1.call-done.from_ref = bf16[512,1024]{1,0:T(8,128)(2,1)} async-done(((bf16[128,1024]{1,0:T(8,128)(2,1)}), bf16[512,1024]{1,0:T(8,128)(2,1)}) %all-gather.3.cloned.1.call-update) | async-done | bytes 1048592 | tf_op jit(solution)/shard_map/all_gather | solution.py:321
  42.2 9.5 %d_hidden.3 = (f32[1,256,3584]{2,1,0:T(8,128)S(1)}, f32[1,256,3584]{2,1,0:T(8,128)}) custom-call(s32[56,8]{1,0:T(8,128)S(1)} %copy.13.m_ref, bf16[512,1024]{1,0:T(8,128)(2,1)S(1)} %ordered.4.x_ref.c_ref, bf16[7168,1024]{1,0:T(8,128)(2,1)} %w_ref.5), custom_call_target="tpu_custom_call" | custom-call | flops 3758096384 | bytes 8388608 | tf_op jit(solution)/shard_map/d_hidden/pallas_call | solution.py:98
  53.5 9.5 %d_hidden.2 = (f32[1,256,3584]{2,1,0:T(8,128)S(1)}, f32[1,256,3584]{2,1,0:T(8,128)}) custom-call(s32[56,8]{1,0:T(8,128)S(1)} %copy.13.m_ref, bf16[512,1024]{1,0:T(8,128)(2,1)S(1)} %ordered.4.x_ref.c_ref, bf16[7168,1024]{1,0:T(8,128)(2,1)} %w_ref.5), custom_call_target="tpu_custom_call" | custom-call | flops 3758096384 | bytes 8388608 | tf_op jit(solution)/shard_map/d_hidden/pallas_call | solution.py:98
  65.4 27.5 %all-gather.5.cloned.1.call-done.from_ref = bf16[512,1024]{1,0:T(8,128)(2,1)} async-done(((bf16[128,1024]{1,0:T(8,128)(2,1)}), bf16[512,1024]{1,0:T(8,128)(2,1)}) %all-gather.5.cloned.1.call-update) | async-done | bytes 1048592 | tf_op jit(solution)/shard_map/all_gather | solution.py:322
  95.0 3.7 add.103
  102.0 15.4 %gate_up.3 = (f32[2,256,3584]{2,1,0:T(8,128)}, f32[2,256,3584]{2,1,0:T(8,128)}) custom-call(s32[8,56]{1,0:T(8,128)S(1)} %copy-done.6, s32[8,56]{1,0:T(8,128)S(1)} %copy-done.7, bf16[512,1024]{1,0:T(8,128)(2,1)S(1)} %ordered.5.x_ref, bf16[1024,7168]{1,0:T(8,128)(2,1)} %g_ref.5, bf16[1024,7168]{1,0:T(8,128)(2,1)} %u_ref.5), custom_call_target="tpu_custom_call" | custom-call | flops 7516192768 | bytes 23068672 | tf_op jit(solution)/shard_map/gate_up/pallas_call | solution.py:73
  117.4 15.4 %gate_up.2 = (f32[2,256,3584]{2,1,0:T(8,128)}, f32[2,256,3584]{2,1,0:T(8,128)}) custom-call(s32[8,56]{1,0:T(8,128)S(1)} %copy-done.6, s32[8,56]{1,0:T(8,128)S(1)} %copy-done.7, bf16[512,1024]{1,0:T(8,128)(2,1)S(1)} %ordered.5.x_ref, bf16[1024,7168]{1,0:T(8,128)(2,1)} %g_ref.5, bf16[1024,7168]{1,0:T(8,128)(2,1)} %u_ref.5), custom_call_target="tpu_custom_call" | custom-call | flops 7516192768 | bytes 23068672 | tf_op jit(solution)/shard_map/gate_up/pallas_call | solution.py:73
  136.2 19.4 %collective-permute-done.2 = bf16[1,2,64,3584]{3,2,1,0:T(8,128)(2,1)S(1)} collective-permute-done((bf16[1,2,64,3584]{3,2,1,0:T(8,128)(2,1)S(1)}, bf16[1,2,64,3584]{3,2,1,0:T(8,128)(2,1)S(1)}, u32[]{:S(2)}, u32[]{:S(2)}) %collective-permute-start.2) | collective-permute-done | bytes 917536 | tf_op jit(solution)/shard_map/ppermute | solution.py:266
  158.8 6.5 %add.113 = f32[2,256,3584]{2,1,0:T(8,128)S(1)} add(f32[2,256,3584]{2,1,0:T(8,128)} %get-tuple-element.33, f32[2,256,3584]{2,1,0:T(8,128)} %collective-permute-done.11) | non-fusion elementwise | flops 1835008 | bytes 22020096 | tf_op jit(solution)/shard_map/add | solution.py:277
  170.8 9.5 %add.106 = f32[2,256,3584]{2,1,0:T(8,128)} add(f32[2,256,3584]{2,1,0:T(8,128)} %get-tuple-element.30, f32[2,256,3584]{2,1,0:T(8,128)} %collective-permute-done.4) | non-fusion elementwise | flops 1835008 | bytes 22020096 | tf_op jit(solution)/shard_map/add | solution.py:277
  183.6 24.4 %collective-permute-done.12 = bf16[2,2,64,3584]{3,2,0,1:T(8,128)(2,1)} collective-permute-done((bf16[2,2,64,3584]{3,2,0,1:T(8,128)(2,1)}, bf16[2,2,64,3584]{3,2,0,1:T(8,128)(2,1)}, u32[]{:S(2)}, u32[]{:S(2)}) %collective-permute-start.12) | collective-permute-done | bytes 1835040 | tf_op jit(solution)/shard_map/ppermute | solution.py:266
  211.5 14.2 %collective-permute-done.5 = bf16[2,2,64,3584]{3,2,0,1:T(8,128)(2,1)S(1)} collective-permute-done((bf16[2,2,64,3584]{3,2,0,1:T(8,128)(2,1)S(1)}, bf16[2,2,64,3584]{3,2,0,1:T(8,128)(2,1)S(1)}, u32[]{:S(2)}, u32[]{:S(2)}) %collective-permute-start.5) | collective-permute-done | bytes 1835040 | tf_op jit(solution)/shard_map/ppermute | solution.py:266
  227.8 14.9 %collective-permute-done.13 = bf16[2,64,3584]{2,1,0:T(8,128)(2,1)S(1)} collective-permute-done((bf16[2,64,3584]{2,1,0:T(8,128)(2,1)S(1)}, bf16[2,64,3584]{2,1,0:T(8,128)(2,1)S(1)}, u32[]{:S(2)}, u32[]{:S(2)}) %collective-permute-start.13) | collective-permute-done | bytes 917536 | tf_op jit(solution)/shard_map/ppermute | solution.py:266
  247.0 6.5 %collective-permute-done.16 = bf16[1,64,3584]{2,1,0:T(8,128)(2,1)S(1)} collective-permute-done((bf16[1,64,3584]{2,1,0:T(8,128)(2,1)S(1)}, bf16[1,64,3584]{2,1,0:T(8,128)(2,1)S(1)}, u32[]{:S(2)}, u32[]{:S(2)}) %collective-permute-start.16) | collective-permute-done | bytes 458784 | tf_op jit(solution)/shard_map/ppermute | solution.py:266
  260.2 14.8 %collective-permute-done.17 = bf16[1,2,64,3584]{3,2,1,0:T(8,128)(2,1)S(1)} collective-permute-done((bf16[1,2,64,3584]{3,2,1,0:T(8,128)(2,1)S(1)}, bf16[1,2,64,3584]{3,2,1,0:T(8,128)(2,1)S(1)}, u32[]{:S(2)}, u32[]{:S(2)}) %collective-permute-start.17) | collective-permute-done | bytes 917536 | tf_op jit(solution)/shard_map/ppermute | solution.py:266
  275.4 5.9 %collective-permute-done.20 = bf16[1,2,64,3584]{3,2,1,0:T(8,128)(2,1)S(1)} collective-permute-done((bf16[1,2,64,3584]{3,2,1,0:T(8,128)(2,1)S(1)}, bf16[1,2,64,3584]{3,2,1,0:T(8,128)(2,1)S(1)}, u32[]{:S(2)}, u32[]{:S(2)}) %collective-permute-start.20) | collective-permute-done | bytes 917536 | tf_op jit(solution)/shard_map/ppermute | solution.py:266
  283.1 10.6 %collective-permute-done.14 = bf16[2,64,3584]{2,1,0:T(8,128)(2,1)S(1)} collective-permute-done((bf16[2,64,3584]{2,1,0:T(8,128)(2,1)S(1)}, bf16[2,64,3584]{2,1,0:T(8,128)(2,1)S(1)}, u32[]{:S(2)}, u32[]{:S(2)}) %collective-permute-start.14) | collective-permute-done | bytes 917536 | tf_op jit(solution)/shard_map/ppermute | solution.py:266
  296.5 8.4 %collective-permute-done.7 = bf16[2,64,3584]{2,1,0:T(8,128)(2,1)S(1)} collective-permute-done((bf16[2,64,3584]{2,1,0:T(8,128)(2,1)S(1)}, bf16[2,64,3584]{2,1,0:T(8,128)(2,1)S(1)}, u32[]{:S(2)}, u32[]{:S(2)}) %collective-permute-start.7) | collective-permute-done | bytes 917536 | tf_op jit(solution)/shard_map/ppermute | solution.py:266
  309.4 24.1 %down_side.1 = (f32[512,1024]{1,0:T(8,128)}, bf16[7168,1024]{1,0:T(8,128)(2,1)}) custom-call(s32[56,8]{1,0:T(8,128)S(1)} %copy.13.m_ref, bf16[512,1024]{1,0:T(8,128)(2,1)S(1)} %ordered.4.x_ref.c_ref, bf16[7168,1024]{1,0:T(8,128)(2,1)} %w_ref.5, bf16[1,256,3584]{2,1,0:T(8,128)(2,1)S(1)} %bitcast.124, ...), custom_call_target="tpu_custom_call" | custom-call | flops 15032385536 | bytes 37748736 | tf_op jit(solution)/shard_map/down_side/pallas_call | solution.py:161
  333.5 10.3 %collective-permute-done.15 = bf16[2,2,64,3584]{3,2,0,1:T(8,128)(2,1)S(1)} collective-permute-done((bf16[2,2,64,3584]{3,2,0,1:T(8,128)(2,1)}, bf16[2,2,64,3584]{3,2,0,1:T(8,128)(2,1)S(1)}, u32[]{:S(2)}, u32[]{:S(2)}) %collective-permute-start.15) | collective-permute-done | bytes 1835040 | tf_op jit(solution)/shard_map/ppermute | solution.py:266
  356.8 5.2 %collective-permute-done.22.rest_1_ = bf16[2,256,3584]{2,1,0:T(8,128)(2,1)} collective-permute-done((bf16[2,256,3584]{2,1,0:T(8,128)(2,1)}, bf16[2,256,3584]{2,1,0:T(8,128)(2,1)}, u32[]{:S(2)}, u32[]{:S(2)}) %collective-permute-start.22) | collective-permute-done | bytes 3670048 | tf_op jit(solution)/shard_map/ppermute | solution.py:266
  362.1 24.9 %d_tokens.1.from_ref = f32[512,1024]{1,0:T(8,128)S(1)} custom-call(s32[8,56]{1,0:T(8,128)S(1)} %copy-done.6, s32[8,56]{1,0:T(8,128)S(1)} %copy-done.7, bf16[1024,7168]{1,0:T(8,128)(2,1)} %g_ref.5, bf16[1024,7168]{1,0:T(8,128)(2,1)} %u_ref.5, bf16[2,256,3584]{2,1,0:T(8,128)(2,1)} %bitcast.39.rest_0_, bf16[2,256,3584]{2,1,0:T(8,128)(2,1)} %collective-permute-done.22.rest_1_, ...), custom_call_target="tpu_custom_call" | custom-call | flops 15032385536 | bytes 44040192 | tf_op jit(solution)/shard_map/d_tokens/pallas_call | solution.py:200
  391.1 25.3 %weight_grads.1 = (bf16[1024,7168]{1,0:T(8,128)(2,1)}, bf16[1024,7168]{1,0:T(8,128)(2,1)}) custom-call(s32[8,56]{1,0:T(8,128)S(1)} %copy-done.6, s32[8,56]{1,0:T(8,128)S(1)} %copy-done.7, bf16[1024,512]{1,0:T(8,128)(2,1)S(1)} %bitcast.125, bf16[2,256,3584]{2,1,0:T(8,128)(2,1)} %bitcast.39.rest_0_, bf16[2,256,3584]{2,1,0:T(8,128)(2,1)} %collective-permute-done.22.rest_1_, ...), custom_call_target="tpu_custom_call" | custom-call | flops 15032385536 | bytes 44040192 | tf_op jit(solution)/shard_map/weight_grads/pallas_call | solution.py:230
  418.1 25.5 %reduce-scatter.5.cloned.1.call-done = f32[128,1024]{1,0:T(8,128)} async-done(((f32[512,1024]{1,0:T(8,128)}), f32[128,1024]{1,0:T(8,128)}) %reduce-scatter.5.cloned.1.call-update) | async-done | bytes 524304 | tf_op jit(solution)/shard_map/reduce_scatter | solution.py:357
  (114 shorter events, 75.0 us)
Async XLA Ops:
  7.2 33.1 %all-gather.3.cloned.1.call-start = ((), (), s32[]{:S(2)}) async-start(), calls=%async_computation.2 | async-start | bytes 1310720 | tf_op jit(solution)/shard_map/all_gather | solution.py:321
  7.9 85.1 %all-gather.5.cloned.1.call-start = ((), (), s32[]{:S(2)}) async-start(), calls=%async_computation.3 | async-start | bytes 1310720 | tf_op jit(solution)/shard_map/all_gather | solution.py:322
  53.5 41.4 %collective-permute-start.1 = (f32[1,256,3584]{2,1,0:T(8,128)}, f32[1,256,3584]{2,1,0:T(8,128)}, u32[]{:S(2)}, u32[]{:S(2)}) collective-permute-start(f32[1,256,3584]{2,1,0:T(8,128)} %get-tuple-element.27), channel_id=1, source_target_pairs={{0,4},{4,0},{8,12},{12,8},{16,20},{20,16},{24,28},{28,24},{1,5},{5... | collective-permute-start | bytes 11010056 | tf_op jit(solution)/shard_map/ppermute | solution.py:266
  64.8 33.9 %collective-permute-start = (f32[1,256,3584]{2,1,0:T(8,128)}, f32[1,256,3584]{2,1,0:T(8,128)}, u32[]{:S(2)}, u32[]{:S(2)}) collective-permute-start(f32[1,256,3584]{2,1,0:T(8,128)} %get-tuple-element.25), channel_id=1, source_target_pairs={{0,4},{4,0},{8,12},{12,8},{16,20},{20,16},{24,28},{28,24},{1,5},{5... | collective-permute-start | bytes 11010056 | tf_op jit(solution)/shard_map/ppermute | solution.py:266
  65.4 351.0 %reduce-scatter.3.cloned.1.call-start = ((), (), s32[]{:S(2)}) async-start(), calls=%async_computation.4 | async-start | bytes 2621440 | tf_op jit(solution)/shard_map/reduce_scatter | solution.py:357
  117.4 41.4 %collective-permute-start.11 = (f32[2,256,3584]{2,1,0:T(8,128)}, f32[2,256,3584]{2,1,0:T(8,128)}, u32[]{:S(2)}, u32[]{:S(2)}) collective-permute-start(f32[2,256,3584]{2,1,0:T(8,128)} %get-tuple-element.34), channel_id=1, source_target_pairs={{0,4},{4,0},{8,12},{12,8},{16,20},{20,16},{24,28},{28,24},{1,5},{5... | collective-permute-start | bytes 22020104 | tf_op jit(solution)/shard_map/ppermute | solution.py:266
  132.8 37.9 %collective-permute-start.4 = (f32[2,256,3584]{2,1,0:T(8,128)}, f32[2,256,3584]{2,1,0:T(8,128)}, u32[]{:S(2)}, u32[]{:S(2)}) collective-permute-start(f32[2,256,3584]{2,1,0:T(8,128)} %get-tuple-element.31), channel_id=1, source_target_pairs={{0,4},{4,0},{8,12},{12,8},{16,20},{20,16},{24,28},{28,24},{1,5},{5... | collective-permute-start | bytes 22020104 | tf_op jit(solution)/shard_map/ppermute | solution.py:266
  133.3 22.3 %collective-permute-start.2 = (bf16[1,2,64,3584]{3,2,1,0:T(8,128)(2,1)S(1)}, bf16[1,2,64,3584]{3,2,1,0:T(8,128)(2,1)S(1)}, u32[]{:S(2)}, u32[]{:S(2)}) collective-permute-start(bf16[1,2,64,3584]{3,2,1,0:T(8,128)(2,1)S(1)} %fusion.8), channel_id=1, source_target_pairs={{0,16},{4,20},{8,24},{12,28},{16,0},{20,4},{24,8},{28,12},{1,17},{... | collective-permute-start | bytes 2752520 | tf_op jit(solution)/shard_map/ppermute | solution.py:266
  134.8 22.7 %collective-permute-start.9 = (bf16[1,2,64,3584]{3,2,1,0:T(8,128)(2,1)S(1)}, bf16[1,2,64,3584]{3,2,1,0:T(8,128)(2,1)S(1)}, u32[]{:S(2)}, u32[]{:S(2)}) collective-permute-start(bf16[1,2,64,3584]{3,2,1,0:T(8,128)(2,1)S(1)} %fusion.11), channel_id=1, source_target_pairs={{0,8},{4,12},{8,0},{12,4},{16,24},{20,28},{24,16},{28,20},{1,9},{5... | collective-permute-start | bytes 2752520 | tf_op jit(solution)/shard_map/ppermute | solution.py:266
  155.9 88.9 %collective-permute-start.3 = (bf16[1,64,3584]{2,1,0:T(8,128)(2,1)S(1)}, bf16[1,64,3584]{2,1,0:T(8,128)(2,1)S(1)}, u32[]{:S(2)}, u32[]{:S(2)}) collective-permute-start(bf16[1,64,3584]{2,1,0:T(8,128)(2,1)S(1)} %fusion.24), channel_id=1, source_target_pairs={{0,8},{4,12},{8,0},{12,4},{16,24},{20,28},{24,16},{28,20},{1,9},{5... | collective-permute-start | bytes 1376264 | tf_op jit(solution)/shard_map/ppermute | solution.py:266
  166.7 41.2 %collective-permute-start.12 = (bf16[2,2,64,3584]{3,2,0,1:T(8,128)(2,1)}, bf16[2,2,64,3584]{3,2,0,1:T(8,128)(2,1)}, u32[]{:S(2)}, u32[]{:S(2)}) collective-permute-start(bf16[2,2,64,3584]{3,2,0,1:T(8,128)(2,1)} %fusion.3), channel_id=1, source_target_pairs={{0,8},{4,12},{8,0},{12,4},{16,24},{20,28},{24,16},{28,20},{1,9},{5... | collective-permute-start | bytes 5505032 | tf_op jit(solution)/shard_map/ppermute | solution.py:266
  169.6 73.3 %collective-permute-start.10 = (bf16[1,64,3584]{2,1,0:T(8,128)(2,1)}, bf16[1,64,3584]{2,1,0:T(8,128)(2,1)S(1)}, u32[]{:S(2)}, u32[]{:S(2)}) collective-permute-start(bf16[1,64,3584]{2,1,0:T(8,128)(2,1)} %fusion.25), channel_id=1, source_target_pairs={{0,16},{4,20},{8,24},{12,28},{16,0},{20,4},{24,8},{28,12},{1,17},{... | collective-permute-start | bytes 1376264 | tf_op jit(solution)/shard_map/ppermute | solution.py:266
  182.7 43.0 %collective-permute-start.5 = (bf16[2,2,64,3584]{3,2,0,1:T(8,128)(2,1)S(1)}, bf16[2,2,64,3584]{3,2,0,1:T(8,128)(2,1)S(1)}, u32[]{:S(2)}, u32[]{:S(2)}) collective-permute-start(bf16[2,2,64,3584]{3,2,0,1:T(8,128)(2,1)S(1)} %fusion.2), channel_id=1, source_target_pairs={{0,16},{4,20},{8,24},{12,28},{16,0},{20,4},{24,8},{28,12},{1,17},{... | collective-permute-start | bytes 5505032 | tf_op jit(solution)/shard_map/ppermute | solution.py:266
  210.0 32.7 %collective-permute-start.13 = (bf16[2,64,3584]{2,1,0:T(8,128)(2,1)S(1)}, bf16[2,64,3584]{2,1,0:T(8,128)(2,1)S(1)}, u32[]{:S(2)}, u32[]{:S(2)}) collective-permute-start(bf16[2,64,3584]{2,1,0:T(8,128)(2,1)S(1)} %fusion.10), channel_id=1, source_target_pairs={{0,16},{4,20},{8,24},{12,28},{16,0},{20,4},{24,8},{28,12},{1,17},{... | collective-permute-start | bytes 2752520 | tf_op jit(solution)/shard_map/ppermute | solution.py:266
  226.3 18.4 %collective-permute-start.6 = (bf16[2,64,3584]{2,1,0:T(8,128)(2,1)S(1)}, bf16[2,64,3584]{2,1,0:T(8,128)(2,1)S(1)}, u32[]{:S(2)}, u32[]{:S(2)}) collective-permute-start(bf16[2,64,3584]{2,1,0:T(8,128)(2,1)S(1)} %fusion.9), channel_id=1, source_target_pairs={{0,8},{4,12},{8,0},{12,4},{16,24},{20,28},{24,16},{28,20},{1,9},{5... | collective-permute-start | bytes 2752520 | tf_op jit(solution)/shard_map/ppermute | solution.py:266
  253.6 21.4 %collective-permute-start.17 = (bf16[1,2,64,3584]{3,2,1,0:T(8,128)(2,1)S(1)}, bf16[1,2,64,3584]{3,2,1,0:T(8,128)(2,1)S(1)}, u32[]{:S(2)}, u32[]{:S(2)}) collective-permute-start(bf16[1,2,64,3584]{3,2,1,0:T(8,128)(2,1)S(1)} %get-tuple-element.56), channel_id=1, source_target_pairs={{0,8},{4,12},{8,0},{12,4},{16,24},{20,28},{24,16},{28,20},{1,9},{5... | collective-permute-start | bytes 2752520 | tf_op jit(solution)/shard_map/ppermute | solution.py:266
  257.9 23.4 %collective-permute-start.20 = (bf16[1,2,64,3584]{3,2,1,0:T(8,128)(2,1)S(1)}, bf16[1,2,64,3584]{3,2,1,0:T(8,128)(2,1)S(1)}, u32[]{:S(2)}, u32[]{:S(2)}) collective-permute-start(bf16[1,2,64,3584]{3,2,1,0:T(8,128)(2,1)S(1)} %get-tuple-element.54), channel_id=1, source_target_pairs={{0,16},{4,20},{8,24},{12,28},{16,0},{20,4},{24,8},{28,12},{1,17},{... | collective-permute-start | bytes 2752520 | tf_op jit(solution)/shard_map/ppermute | solution.py:266
  259.9 33.7 %collective-permute-start.14 = (bf16[2,64,3584]{2,1,0:T(8,128)(2,1)S(1)}, bf16[2,64,3584]{2,1,0:T(8,128)(2,1)S(1)}, u32[]{:S(2)}, u32[]{:S(2)}) collective-permute-start(bf16[2,64,3584]{2,1,0:T(8,128)(2,1)S(1)} %get-tuple-element.58), channel_id=1, source_target_pairs={{0,16},{4,20},{8,24},{12,28},{16,0},{20,4},{24,8},{28,12},{1,17},{... | collective-permute-start | bytes 2752520 | tf_op jit(solution)/shard_map/ppermute | solution.py:266
  275.3 32.9 %collective-permute-start.18 = (bf16[1,256,3584]{2,1,0:T(8,128)(2,1)S(1)}, bf16[1,256,3584]{2,1,0:T(8,128)(2,1)S(1)}, u32[]{:S(2)}, u32[]{:S(2)}) collective-permute-start(bf16[1,256,3584]{2,1,0:T(8,128)(2,1)S(1)} %bitcast.123), channel_id=1, source_target_pairs={{0,4},{4,0},{8,12},{12,8},{16,20},{20,16},{24,28},{28,24},{1,5},{5... | collective-permute-start | bytes 5505032 | tf_op jit(solution)/shard_map/ppermute | solution.py:266
  281.5 26.7 %collective-permute-start.21 = (bf16[1,256,3584]{2,1,0:T(8,128)(2,1)S(1)}, bf16[1,256,3584]{2,1,0:T(8,128)(2,1)S(1)}, u32[]{:S(2)}, u32[]{:S(2)}) collective-permute-start(bf16[1,256,3584]{2,1,0:T(8,128)(2,1)S(1)} %bitcast.138), channel_id=1, source_target_pairs={{0,4},{4,0},{8,12},{12,8},{16,20},{20,16},{24,28},{28,24},{1,5},{5... | collective-permute-start | bytes 5505032 | tf_op jit(solution)/shard_map/ppermute | solution.py:266
  281.7 23.2 %collective-permute-start.7 = (bf16[2,64,3584]{2,1,0:T(8,128)(2,1)S(1)}, bf16[2,64,3584]{2,1,0:T(8,128)(2,1)S(1)}, u32[]{:S(2)}, u32[]{:S(2)}) collective-permute-start(bf16[2,64,3584]{2,1,0:T(8,128)(2,1)S(1)} %get-tuple-element.60), channel_id=1, source_target_pairs={{0,8},{4,12},{8,0},{12,4},{16,24},{20,28},{24,16},{28,20},{1,9},{5... | collective-permute-start | bytes 2752520 | tf_op jit(solution)/shard_map/ppermute | solution.py:266
  295.2 48.6 %collective-permute-start.15 = (bf16[2,2,64,3584]{3,2,0,1:T(8,128)(2,1)}, bf16[2,2,64,3584]{3,2,0,1:T(8,128)(2,1)S(1)}, u32[]{:S(2)}, u32[]{:S(2)}) collective-permute-start(bf16[2,2,64,3584]{3,2,0,1:T(8,128)(2,1)} %get-tuple-element.50), channel_id=1, source_target_pairs={{0,8},{4,12},{8,0},{12,4},{16,24},{20,28},{24,16},{28,20},{1,9},{5... | collective-permute-start | bytes 5505032 | tf_op jit(solution)/shard_map/ppermute | solution.py:266
  306.4 41.5 %collective-permute-start.8 = (bf16[2,2,64,3584]{3,2,1,0:T(8,128)(2,1)}, bf16[2,2,64,3584]{3,2,1,0:T(8,128)(2,1)S(1)}, u32[]{:S(2)}, u32[]{:S(2)}) collective-permute-start(bf16[2,2,64,3584]{3,2,1,0:T(8,128)(2,1)} %get-tuple-element.48), channel_id=1, source_target_pairs={{0,16},{4,20},{8,24},{12,28},{16,0},{20,4},{24,8},{28,12},{1,17},{... | collective-permute-start | bytes 5505032 | tf_op jit(solution)/shard_map/ppermute | solution.py:266
  354.2 89.4 %reduce-scatter.5.cloned.1.call-start = ((), (), s32[]{:S(2)}) async-start(), calls=%async_computation.5 | async-start | bytes 2621440 | tf_op jit(solution)/shard_map/reduce_scatter | solution.py:357
  (17 other events, 179.6 us)
Sparse Core Ops, SparseCore 0:
  9.6 30.6 all-gather.2
  65.5 27.4 all-gather.4
  354.3 43.7 reduce-scatter.2
  400.4 43.1 reduce-scatter.4
